TPU v7x, 512 devices: a whole 4x8x8 slice. The times are simulated.
512 devices in a mesh: pipe: 64 (over x, z_hi, y), head: 8 (over z_lo, core).
Axes of the slice: x: 4, y: 8, z: 8 (z_hi: 2, z_lo: 4; z = z_hi * 4 + z_lo), core: 2. Of those that a mesh axis runs over, the one named last changes fastest.
Arguments:
- fresh_qkv: bfloat16 [8192, 9216], P(('pipe', 'head')), may hold values from -6 to 6
- stale_kv: bfloat16 [2, 8192, 3072], P(None, 'pipe', 'head'), may hold values from -20 to 20
- text_kv: bfloat16 [2, 512, 3072], P(None, None, 'head'), may hold values from -12 to 12
- text_len: int32 [1], replicated, may hold values from 64 to 512
- q_gain: float32 [128], replicated, may hold values from 0.5 to 3
- k_gain: float32 [128], replicated, may hold values from 0.5 to 3
- out_weight: bfloat16 [3072, 3072], P('head'), may hold values from -0.15625 to 0.15625
- hidden: bfloat16 [8192, 3072], P(('pipe', 'head')), may hold values from -0.796875 to 0.796875
- gate: float32 [3072], replicated, may hold values from 1 to 8
Outputs:
- updated: bfloat16 [8192, 3072], P(('pipe', 'head'))
All inputs are finite; a program needn't handle non-finite values.
Results may differ from a plain program's by a relative error of at most 0.0082.
Values may be sent and summed in bfloat16 or wider, within the bound.
A program may use at most 64 MiB of HBM per device.

v0:
```python
import math

import jax
import jax.numpy as jnp
from jax import lax
from jax.sharding import PartitionSpec as P

HEAD_DIM = 128


def rms_scale(values, gain):
    mean_sq = jnp.mean(values * values, axis=-1, keepdims=True)
    return values * lax.rsqrt(mean_sq + 1e-06) * gain


def on_device(fresh_qkv, stale_kv, text_kv, text_len, q_gain, k_gain, out_weight, hidden, gate):
    rows = fresh_qkv.shape[0]
    heads_all = fresh_qkv.shape[1] // (3 * HEAD_DIM)
    split = fresh_qkv.reshape(rows, 3, heads_all, HEAD_DIM)
    local = lax.all_to_all(split, "head", split_axis=2, concat_axis=0, tiled=True)
    patch = local.shape[0]
    heads_dev = local.shape[2]
    queries = rms_scale(local[:, 0].astype(jnp.float32), q_gain).astype(jnp.bfloat16)
    queries = jnp.transpose(queries, (1, 0, 2))
    fresh_keys = rms_scale(local[:, 1].astype(jnp.float32), k_gain).astype(jnp.bfloat16)
    fresh_values = local[:, 2]
    scale = HEAD_DIM ** (-0.5)

    def attend(state, keys, values, valid):
        top, total, summed = state
        scores = (
            jnp.einsum("hqd,khd->hqk", queries, keys, preferred_element_type=jnp.float32) * scale
        )
        scores = jnp.where(valid[None, None, :], scores, -1e30)
        new_top = jnp.maximum(top, jnp.max(scores, axis=-1))
        expo = jnp.exp(scores - new_top[:, :, None])
        shrink = jnp.exp(top - new_top)
        total = total * shrink + jnp.sum(expo, axis=-1)
        update = jnp.einsum(
            "hqk,khd->hqd", expo.astype(jnp.bfloat16), values, preferred_element_type=jnp.float32
        )
        return (new_top, total, summed * shrink[:, :, None] + update)

    state = (
        jnp.full((heads_dev, patch), -1e30, jnp.float32),
        jnp.zeros((heads_dev, patch), jnp.float32),
        jnp.zeros((heads_dev, patch, HEAD_DIM), jnp.float32),
    )
    text_rows = text_kv.shape[1]
    text_valid = jnp.arange(text_rows, dtype=jnp.int32) < text_len[0]
    state = attend(
        state,
        text_kv[0].reshape(text_rows, heads_dev, HEAD_DIM),
        text_kv[1].reshape(text_rows, heads_dev, HEAD_DIM),
        text_valid,
    )
    state = attend(state, fresh_keys, fresh_values, jnp.ones((patch,), bool))
    own = lax.axis_index("pipe") * patch

    def fold_piece(carry, piece, start):
        count = piece.shape[1]
        positions = start + jnp.arange(count, dtype=jnp.int32)
        valid = (positions < own) | (positions >= own + patch)
        return attend(
            carry,
            piece[0].reshape(count, heads_dev, HEAD_DIM),
            piece[1].reshape(count, heads_dev, HEAD_DIM),
            valid,
        )

    whole = lax.all_gather(stale_kv, "pipe", axis=1, tiled=True)
    sections = lax.axis_size("pipe")
    block = patch * math.gcd(sections, max(1, 1024 // patch))
    count = whole.shape[1] // block
    pieces = jnp.transpose(whole.reshape(2, count, block, whole.shape[2]), (1, 0, 2, 3))
    starts = jnp.arange(count, dtype=jnp.int32) * block

    def scan_step(carry, item):
        return (fold_piece(carry, item[0], item[1]), None)

    state = lax.scan(scan_step, state, (pieces, starts))[0]
    top, total, summed = state
    attn = (summed / total[:, :, None]).astype(jnp.bfloat16)
    attn = jnp.transpose(attn, (1, 0, 2)).reshape(patch, heads_dev * HEAD_DIM)
    partial_out = lax.psum_scatter(
        jnp.dot(attn, out_weight, preferred_element_type=jnp.float32),
        "head",
        scatter_dimension=0,
        tiled=True,
    )
    return (hidden.astype(jnp.float32) + gate * partial_out).astype(jnp.bfloat16)


def solution(mesh):
    return jax.shard_map(
        on_device,
        mesh=mesh,
        in_specs=(
            P(("pipe", "head"), None),
            P(None, "pipe", "head"),
            P(None, None, "head"),
            P(),
            P(),
            P(),
            P("head", None),
            P(("pipe", "head"), None),
            P(),
        ),
        out_specs=P(("pipe", "head"), None),
        check_vma=False,
    )
```

profile of v0, /device:TPU:1, one launch (start us, length us, event | category | flops | bytes accessed | tf_op | source)
XLA Modules:
  0.0 380.7 jit_solution(12929610768092136224)
XLA Ops:
  9.0 10.2 %all-to-all-start = ((bf16[16,3,24,128]{3,0,1,2:T(8,128)(2,1)}), bf16[16,3,24,128]{3,0,1,2:T(8,128)(2,1)S(1)}, u32[]{:S(2)}, u32[]{:S(2)}) async-start(bf16[16,3,24,128]{3,0,1,2:T(8,128)(2,1)} %copy.51), calls=%async_computation | async-start | bytes 589824 | tf_op jit(solution)/shard_map/all_to_all | solution.py:20
  19.9 2.0 fusion.29
  23.2 5.4 %all-to-all-done = bf16[16,3,24,128]{3,0,1,2:T(8,128)(2,1)S(1)} async-done(((bf16[16,3,24,128]{3,0,1,2:T(8,128)(2,1)}), bf16[16,3,24,128]{3,0,1,2:T(8,128)(2,1)S(1)}, u32[]{:S(2)}, u32[]{:S(2)}) %all-to-all-start) | async-done | bytes 294944 | tf_op jit(solution)/shard_map/all_to_all | solution.py:20
  30.5 234.8 %all-gather.2.cloned.1.call-done = bf16[2,8192,384]{2,1,0:T(8,128)(2,1)} async-done(((bf16[2,128,384]{2,1,0:T(8,128)(2,1)}), bf16[2,8192,384]{2,1,0:T(8,128)(2,1)}) %all-gather.2.cloned.1.call-update) | async-done | bytes 12582928 | tf_op jit(solution)/shard_map/all_gather | solution.py:71
  265.3 70.5 %while.15 = (s32[]{:T(128)}, f32[3,128]{1,0:T(4,128)S(1)}, f32[3,128]{1,0:T(4,128)S(1)}, f32[3,128,128]{2,1,0:T(8,128)S(1)}, s32[8]{0:T(128)S(1)}, /*index=5*/s3...) while((s32[]{:T(128)}, f32[3,128]{1,0:T(4,128)S(1)}, ...), condition=%wide.region_9.10_spmd, body=%wide.region_6.9_spmd.sunk | while | flops 204182272 | bytes 13101225 | solution.py:81
  266.5 2.5 constant_dynamic-slice_fusion.3
  270.2 1.4 copy.77
  271.6 1.7 bitcast_reduce_fusion.2
  275.4 2.5 constant_dynamic-slice_fusion.3
  279.0 1.4 copy.77
  280.4 1.7 bitcast_reduce_fusion.2
  284.2 2.5 constant_dynamic-slice_fusion.3
  287.8 1.4 copy.77
  289.2 1.7 bitcast_reduce_fusion.2
  293.0 2.5 constant_dynamic-slice_fusion.3
  296.6 1.4 copy.77
  298.0 1.7 bitcast_reduce_fusion.2
  301.8 2.5 constant_dynamic-slice_fusion.3
  305.4 1.4 copy.77
  306.8 1.7 bitcast_reduce_fusion.2
  310.6 2.5 constant_dynamic-slice_fusion.3
  314.2 1.4 copy.77
  315.6 1.7 bitcast_reduce_fusion.2
  319.4 2.5 constant_dynamic-slice_fusion.3
  323.0 1.4 copy.77
  324.5 1.7 bitcast_reduce_fusion.2
  328.2 2.5 constant_dynamic-slice_fusion.3
  331.9 1.4 copy.77
  333.3 1.7 bitcast_reduce_fusion.2
  336.0 1.8 fusion.32
  337.8 34.5 %reduce-scatter.2.cloned.1.call-done = f32[16,3072]{1,0:T(8,128)} async-done(((f32[128,3072]{1,0:T(8,128)}), f32[16,3072]{1,0:T(8,128)}) %reduce-scatter.2.cloned.1.call-update) | async-done | bytes 196624 | tf_op jit(solution)/shard_map/reduce_scatter | solution.py:85
  372.3 1.6 add_convert_fusion
  (99 shorter events, 31.1 us)
Async XLA Ops:
  6.5 329.4 %copy-start = (bf16[384,3072]{1,0:T(8,128)(2,1)S(1)}, bf16[384,3072]{1,0:T(8,128)(2,1)}, u32[]{:S(2)}) copy-start(bf16[384,3072]{1,0:T(8,128)(2,1)} %param.17) | copy-start | bytes 7077892
  6.5 258.8 %all-gather.2.cloned.1.call-start = ((), (), s32[]{:S(2)}) async-start(), calls=%async_computation.2 | async-start | bytes 12779520 | tf_op jit(solution)/shard_map/all_gather | solution.py:71
  9.0 19.6 %all-to-all-start = ((bf16[16,3,24,128]{3,0,1,2:T(8,128)(2,1)}), bf16[16,3,24,128]{3,0,1,2:T(8,128)(2,1)S(1)}, u32[]{:S(2)}, u32[]{:S(2)}) async-start(bf16[16,3,24,128]{3,0,1,2:T(8,128)(2,1)} %copy.51), calls=%async_computation | async-start | bytes 589824 | tf_op jit(solution)/shard_map/all_to_all | solution.py:20
  19.2 353.0 %reduce-scatter.2.cloned.1.call-start = ((), (), s32[]{:S(2)}) async-start(), calls=%async_computation.3 | async-start | bytes 1769472 | tf_op jit(solution)/shard_map/reduce_scatter | solution.py:85
  21.9 7.0 %copy-start.3 = (f32[128]{0:T(128)S(1)}, f32[128]{0:T(128)}, u32[]{:S(2)}) copy-start(f32[128]{0:T(128)} %param.15) | copy-start | bytes 1540
  21.9 7.1 %copy-start.4 = (f32[128]{0:T(128)S(1)}, f32[128]{0:T(128)}, u32[]{:S(2)}) copy-start(f32[128]{0:T(128)} %param.16) | copy-start | bytes 1540
  337.7 34.5 %copy-start.1 = (bf16[16,3072]{1,0:T(8,128)(2,1)S(1)}, bf16[16,3072]{1,0:T(8,128)(2,1)}, u32[]{:S(2)}) copy-start(bf16[16,3072]{1,0:T(8,128)(2,1)} %param.18) | copy-start | bytes 294916
  337.7 34.5 %copy-start.2 = (f32[3072]{0:T(1024)S(1)}, f32[3072]{0:T(1024)}, u32[]{:S(2)}) copy-start(f32[3072]{0:T(1024)} %param.19) | copy-start | bytes 36868
Sparse Core Ops, SparseCore 0:
  11.9 253.3 all-gather.1
  337.9 34.3 reduce-scatter.1
where the time goes:
time: 384 us; the launch traced here: 381 us
  waiting for transfers between devices  275 us (72%)
  local copies, waits for them, and re-layouts  50.5 us (13%)
  matrix products  20.9 us (5%)
  between operations  14.2 us (4%)
  starting transfers between devices  10.2 us (3%)
  other arithmetic  9.15 us (2%)
    all_gather x1, waiting for transfers between devices, on_device(): whole = lax.all_gather(stale_kv, 'pipe', axis=1, tiled=True)  235 us
    reduce_scatter x1, waiting for transfers between devices, on_device(): lax.psum_scatter(jnp.dot(attn, out_weight, preferred_element_type=jnp.flo...  34.5 us
    while x24, local copies, waits for them, and re-layouts  20.6 us
    slice x8, local copies, waits for them, and re-layouts, fold_piece(): piece[1].reshape(count, heads_dev, HEAD_DIM)  19.7 us
    dot_general x10, matrix products, attend(): jnp.einsum('hqd,khd->hqk', queries, keys, preferred_element_type=jnp.floa...  14.5 us
    all_to_all x1, starting transfers between devices, on_device(): lax.all_to_all(split, 'head', split_axis=2, concat_axis=0, tiled=True)  10.2 us
  transfers between devices with their start and end apart: 3, of which 3 were waited for; matrix products, arithmetic and copies ran while one was open for 2% of the time, Pallas kernels for 0%

commit v1 on v0

v1 whole, which is shorter than its diff:
```python
import math

import jax
import jax.numpy as jnp
from jax import lax
from jax.experimental import pallas as pl
from jax.experimental.pallas import tpu as pltpu
from jax.sharding import PartitionSpec as P

MESH = pl.DeviceIdType.MESH
HD = 128
HEADS = 3
W = HEADS * HD
PATCH = 128
NX, NZ, NY, NL, NC = 4, 2, 8, 4, 2
NH = NL * NC
TOK = PATCH // NH
OWN = NY
D = 3072
CHUNKS = 3
CW = D // CHUNKS
BF, F32 = jnp.bfloat16, jnp.float32


def dot_nt(a, b):
    return lax.dot_general(a, b, (((1,), (1,)), ((), ())), preferred_element_type=F32)


def spread_rows(column):
    return jnp.transpose(jnp.broadcast_to(column, (PATCH, HD)))[0:8]


def split_three(rows):
    hi = rows.astype(BF).astype(F32)
    rest = rows - hi
    mid = rest.astype(BF).astype(F32)
    low = rest - mid
    at = lax.broadcasted_iota(jnp.int32, rows.shape, 0)
    return jnp.where(at == 0, hi, jnp.where(at == 1, mid, jnp.where(at == 2, low, 0.0)))


def merge(parts, logs):
    top = logs[0]
    for row in logs[1:]:
        top = jnp.maximum(top, row)
    shares = [jnp.exp2(row - top) for row in logs]
    total = shares[0]
    for share in shares[1:]:
        total = total + share
    inverse = 1.0 / total
    at = lax.broadcasted_iota(jnp.int32, (8, HD), 0)
    packed = jnp.zeros((8, HD), F32)
    for i, share in enumerate(shares):
        packed = jnp.where(at == i, share * inverse, packed)
    columns = jnp.transpose(jnp.concatenate([packed] * (PATCH // 8), axis=0))
    out = columns[:, 0:1] * parts[0]
    for i in range(1, len(parts)):
        out = out + columns[:, i : i + 1] * parts[i]
    return out, top + jnp.log2(total)


def kernel(
    fresh, stale, text, tlen, qg, kg, w, hidden, gate, o_ref,
    qraw, kvraw, qall, kv, txt, obuf, orecv, zown, zlog, zsend, zrecv, attn, wv, psend, pown, precv, rsend, rrecv,
    loc_sem, q_ssem, q_rsem, f_ssem, f_rsem, kv_ssem, kv_rsem, x_ssem, x_rsem, o_ssem, o_rsem, z_ssem, z_rsem,
    p_ssem, p_rsem, r_ssem, r_rsem,
):
    pipe, me = lax.axis_index("pipe"), lax.axis_index("head")
    x, zh, y = pipe // (NZ * NY), (pipe // NY) % NZ, pipe % NY
    zl, core = me // NC, me % NC

    def at_x(j):
        return ((((x + j) % NX) * NZ + zh) * NY + y, me)

    def at_y(j):
        return ((x * NZ + zh) * NY + (y + j) % NY, me)

    def at_head(r, i):
        return ((x * NZ + (zh + r) % NZ) * NY + y, (me + i) % NH)

    def at_zl(i):
        return (pipe, ((zl + i) % NL) * NC + core)

    pair = (pipe, zl * NC + 1 - core)

    def remote(src, dst, ssem, rsem, dev):
        return pltpu.make_async_remote_copy(
            src_ref=src, dst_ref=dst, send_sem=ssem, recv_sem=rsem, device_id=dev, device_id_type=MESH
        )

    share = x * NZ + zh
    locals_ = [
        pltpu.make_async_copy(w, wv, loc_sem.at[0]),
        pltpu.make_async_copy(
            text.at[:, pl.ds(pl.multiple_of((share // 2) * 128, 128), 128), :], txt, loc_sem.at[1]
        ),
    ]
    own_copies = [
        pltpu.make_async_copy(
            stale.at[:, :, pl.ds(h * HD, HD)], kv.at[h, OWN], loc_sem.at[2 + h]
        )
        for h in range(HEADS)
    ]
    for copy in own_copies + locals_:
        copy.start()

    bar = pltpu.get_barrier_semaphore()
    partners = [at_x(j) for j in range(1, NX)] + [at_y(1), at_y(NY - 1)]
    partners += [at_head(r, i) for r in range(NZ) for i in range(NH) if (r, i) != (0, 0)]
    for dev in partners:
        pl.semaphore_signal(bar, inc=1, device_id=dev, device_id_type=MESH)
    pl.semaphore_wait(bar, len(partners))

    def head_cols(part, i):
        return fresh.at[:, pl.ds(pl.multiple_of(part * D + ((me + i) % NH) * W, W), W)]

    def q_hop(r, i):
        return remote(head_cols(0, i), qraw.at[r, i], q_ssem.at[r, i], q_rsem.at[r, i], at_head(r, i))

    def f_hop(part, i):
        return remote(head_cols(part + 1, i), kvraw.at[part, i], f_ssem.at[part, i], f_rsem.at[part, i], at_head(0, i))

    q_local = pltpu.make_async_copy(head_cols(0, 0), qraw.at[0, 0], q_rsem.at[0, 0])
    f_local = [
        pltpu.make_async_copy(head_cols(part + 1, 0), kvraw.at[part, 0], f_rsem.at[part, 0])
        for part in range(2)
    ]

    q_local.start()
    for r in range(NZ):
        for i in range(NH):
            if (r, i) != (0, 0):
                q_hop(r, i).start()

    def hop(h, slot):
        if slot == 1 or slot == NY - 1:
            src = stale.at[:, :, pl.ds(h * HD, HD)]
        elif slot == 40:
            src = kv.at[h, 3, 0]
        elif slot == 41:
            src = kv.at[h, 5, 1]
        else:
            src = kv.at[h, slot - 1 if slot < 4 else slot + 1]
        if slot >= 40:
            dst = kv.at[h, 4, slot - 40]
        else:
            dst = kv.at[h, slot]
        sem = {40: 0, 41: 4}.get(slot, slot)
        up = slot < 4 or slot == 40
        return remote(src, dst, kv_ssem.at[h, sem], kv_rsem.at[h, sem], at_y(1 if up else NY - 1))

    for h in range(HEADS):
        hop(h, 1).start()
        hop(h, 7).start()

    for part in range(2):
        f_local[part].start()
        for i in range(1, NH):
            f_hop(part, i).start()

    for h in range(HEADS):
        hop(h, 1).wait_recv()
        hop(h, 2).start()
        hop(h, 7).wait_recv()
        hop(h, 6).start()

    scale = math.log2(math.e) / math.sqrt(HD)
    q_local.wait()
    for r in range(NZ):
        for i in range(NH):
            if (r, i) != (0, 0):
                q_hop(r, i).wait_recv()

    def x_hop(h, j):
        return remote(qall.at[h, 0], qall.at[h, NX - j], x_ssem.at[h, j], x_rsem.at[h, NX - j], at_x(j))

    for h in range(HEADS):
        for r in range(NZ):
            q = qraw[r, :, :, pl.ds(h * HD, HD)].reshape(PATCH, HD).astype(F32)
            q = q * lax.rsqrt(jnp.mean(q * q, axis=-1, keepdims=True) + 1e-06)
            qall[h, 0, pl.ds(r * PATCH, PATCH), :] = (q * qg[...]).astype(BF)
        for j in (1, 3, 2):
            x_hop(h, j).start()

    for h in range(HEADS):
        hop(h, 2).wait_recv()
        hop(h, 3).start()
        hop(h, 6).wait_recv()
        hop(h, 5).start()

    for part in range(2):
        f_local[part].wait()
        for i in range(1, NH):
            f_hop(part, i).wait_recv()
    for h in range(HEADS):
        k = kvraw[0, :, :, pl.ds(h * HD, HD)].reshape(PATCH, HD).astype(F32)
        k = k * lax.rsqrt(jnp.mean(k * k, axis=-1, keepdims=True) + 1e-06)
        kv[h, 0, 0] = (k * kg[...]).astype(BF)
        kv[h, 0, 1] = kvraw[1, :, :, pl.ds(h * HD, HD)].reshape(PATCH, HD)

    for h in range(HEADS):
        hop(h, 3).wait_recv()
        hop(h, 40).start()
        hop(h, 5).wait_recv()
        hop(h, 41).start()

    for copy in own_copies:
        copy.wait()
    locals_[1].wait()
    spot = lax.broadcasted_iota(jnp.int32, (1, 128), 1)
    live = (spot // 64 == share % 2) & (spot + (share // 2) * 128 < tlen[0])
    bias = jnp.where(live, 0.0, -1e30)

    def o_hop(h, j):
        return remote(obuf.at[h, j], orecv.at[h, NX - j], o_ssem.at[h, j], o_rsem.at[h, NX - j], at_x(j))

    def z_hop(h):
        return remote(zsend.at[h], zrecv.at[h], z_ssem.at[h], z_rsem.at[h], at_head(1, 0))

    def attend(h, t):
        j = (t + 1) % NX
        stats = []
        for r in range(NZ):
            slots = pl.ds(1 - t // (NX - 1) if r == 0 else 1, NY)
            q = qall[h, j, pl.ds(r * PATCH, PATCH), :]
            scores = dot_nt(q, kv[h, slots, 0].reshape(NY * PATCH, HD))
            tscores = dot_nt(q, txt[0, :, pl.ds(h * HD, HD)]) + bias
            top = jnp.maximum(jnp.max(scores, axis=-1, keepdims=True), jnp.max(tscores, axis=-1, keepdims=True))
            e, te = jnp.exp2((scores - top) * scale), jnp.exp2((tscores - top) * scale)
            total = jnp.sum(e, axis=-1, keepdims=True) + jnp.sum(te, axis=-1, keepdims=True)
            out = jnp.dot(e.astype(BF), kv[h, slots, 1].reshape(NY * PATCH, HD), preferred_element_type=F32)
            out = out + jnp.dot(te.astype(BF), txt[1, :, pl.ds(h * HD, HD)], preferred_element_type=F32)
            obuf[h, j, pl.ds(r * PATCH, PATCH), :] = (out * (1.0 / total)).astype(BF)
            stats.append(split_three(spread_rows(top * scale + jnp.log2(total))))
        obuf[h, j, pl.ds(NZ * PATCH, 16), :] = jnp.concatenate(stats, axis=0).astype(BF)

    def logs_of(packed, r):
        rows = packed.astype(F32)
        return rows[8 * r : 8 * r + 1] + rows[8 * r + 1 : 8 * r + 2] + rows[8 * r + 2 : 8 * r + 3]

    def combine_x(h):
        for j in range(1, NX):
            o_hop(h, j).wait_recv()
        sources = [obuf.at[h, 0]] + [orecv.at[h, j] for j in range(1, NX)]
        for r in (1, 0):
            parts = [s[pl.ds(r * PATCH, PATCH), :].astype(F32) for s in sources]
            logs = [logs_of(s[pl.ds(NZ * PATCH, 16), :], r) for s in sources]
            out, log = merge(parts, logs)
            if r == 1:
                zsend[h, pl.ds(0, PATCH), :] = out.astype(BF)
                packed = split_three(jnp.broadcast_to(log, (8, HD)))
                zsend[h, pl.ds(PATCH, 16), :] = jnp.concatenate([packed, packed], axis=0).astype(BF)
                z_hop(h).start()
            else:
                zown[h] = out
                zlog[h] = jnp.broadcast_to(log, (8, HD))

    for h in range(HEADS):
        for j in range(1, NX):
            x_hop(h, j).wait_recv()
        hop(h, 40).wait_recv()
        hop(h, 41).wait_recv()

        for t in range(NX):
            attend(h, t)
            if t < NX - 1:
                o_hop(h, t + 1).start()
        if h > 0:
            combine_x(h - 1)
    combine_x(HEADS - 1)

    for h in range(HEADS):
        z_hop(h).wait_recv()
        out, _ = merge(
            [zown[h], zrecv[h, pl.ds(0, PATCH), :].astype(F32)],
            [zlog[h, 0:1], logs_of(zrecv[h, pl.ds(PATCH, 16), :], 0)],
        )
        attn[:, :, pl.ds(h * HD, HD)] = out.astype(BF).reshape(NH, TOK, HD)

    locals_[0].wait()
    rows = jnp.concatenate(
        [attn[(me + NH - ((zl + i) % NL) * NC - c) % NH] for c in (1 - core, core) for i in range(NL)], axis=0
    )

    def p_hop(c):
        return remote(psend.at[c], precv.at[c], p_ssem.at[c], p_rsem.at[c], pair)

    def r_hop(c, i):
        return remote(rsend.at[c, i], rrecv.at[c, NL - i], r_ssem.at[c, i], r_rsem.at[c, NL - i], at_zl(i))

    half = NL * TOK
    for c in range(CHUNKS):
        cols = pl.ds(c * CW, CW)
        part = jnp.dot(rows, wv[:, cols], preferred_element_type=F32)
        psend[c] = part[:half].astype(BF)
        p_hop(c).start()
        pown[c] = part[half:]
    for c in range(CHUNKS):
        p_hop(c).wait_recv()
        both = pown[c] + precv[c].astype(F32)
        for i in (2, 1, 3):
            rsend[c, i] = both[i * TOK : (i + 1) * TOK].astype(BF)
            r_hop(c, i).start()
        pown[c, pl.ds(0, TOK), :] = both[:TOK]
    for c in range(CHUNKS):
        cols = pl.ds(c * CW, CW)
        total = pown[c, pl.ds(0, TOK), :]
        for i in range(1, NL):
            r_hop(c, NL - i).wait_recv()
            total = total + rrecv[c, i].astype(F32)
        o_ref[:, cols] = (hidden[:, cols].astype(F32) + gate[:, cols] * total).astype(BF)

    for r in range(2):
        for i in range(NH):
            if (r, i) != (0, 0):
                q_hop(r, i).wait_send()
            if i > 0:
                f_hop(r, i).wait_send()
    for h in range(HEADS):
        for slot in (1, 2, 3, 40, 41, 5, 6, 7):
            hop(h, slot).wait_send()
        for j in range(1, NX):
            x_hop(h, j).wait_send()
            o_hop(h, j).wait_send()
        z_hop(h).wait_send()
    for c in range(CHUNKS):
        p_hop(c).wait_send()
        for i in range(1, NL):
            r_hop(c, i).wait_send()


def on_device(fresh, stale, text, tlen, qg, kg, w, hidden, gate):
    dma = pltpu.SemaphoreType.DMA
    hbm, vmem = pl.BlockSpec(memory_space=pl.ANY), pl.BlockSpec(memory_space=pltpu.VMEM)
    return pl.pallas_call(
        kernel,
        out_shape=jax.ShapeDtypeStruct((TOK, D), BF),
        in_specs=[hbm, hbm, hbm, pl.BlockSpec(memory_space=pltpu.SMEM), vmem, vmem, hbm, vmem, vmem],
        out_specs=vmem,
        scratch_shapes=[
            pltpu.VMEM((NZ, NH, TOK, W), BF),
            pltpu.VMEM((2, NH, TOK, W), BF),
            pltpu.VMEM((HEADS, NX, NZ * PATCH, HD), BF),
            pltpu.VMEM((HEADS, NY + 1, 2, PATCH, HD), BF),
            pltpu.VMEM((2, 128, W), BF),
            pltpu.VMEM((HEADS, NX, NZ * PATCH + 16, HD), BF),
            pltpu.VMEM((HEADS, NX, NZ * PATCH + 16, HD), BF),
            pltpu.VMEM((HEADS, PATCH, HD), F32),
            pltpu.VMEM((HEADS, 8, HD), F32),
            pltpu.VMEM((HEADS, PATCH + 16, HD), BF),
            pltpu.VMEM((HEADS, PATCH + 16, HD), BF),
            pltpu.VMEM((NH, TOK, W), BF),
            pltpu.VMEM((W, D), BF),
            pltpu.VMEM((CHUNKS, NL * TOK, CW), BF),
            pltpu.VMEM((CHUNKS, NL * TOK, CW), F32),
            pltpu.VMEM((CHUNKS, NL * TOK, CW), BF),
            pltpu.VMEM((CHUNKS, NL, TOK, CW), BF),
            pltpu.VMEM((CHUNKS, NL, TOK, CW), BF),
            dma((2 + HEADS,)), dma((NZ, NH)), dma((NZ, NH)), dma((2, NH)), dma((2, NH)), dma((HEADS, NY)), dma((HEADS, NY)),
            dma((HEADS, NX)), dma((HEADS, NX)), dma((HEADS, NX)), dma((HEADS, NX)), dma((HEADS,)), dma((HEADS,)),
            dma((CHUNKS,)), dma((CHUNKS,)), dma((CHUNKS, NL)), dma((CHUNKS, NL)),
        ],
        name="joint_attention",
        cost_estimate=pl.CostEstimate(flops=2 * 10**9, bytes_accessed=4 * 10**6, transcendentals=4 * 10**6),
        compiler_params=pltpu.CompilerParams(
            collective_id=0, has_side_effects=True, vmem_limit_bytes=60 * 2**20
        ),
    )(fresh, stale, text, tlen, qg.reshape(1, HD), kg.reshape(1, HD), w, hidden, gate.reshape(1, D))


def solution(mesh):
    return jax.shard_map(
        on_device,
        mesh=mesh,
        in_specs=(
            P(("pipe", "head"), None),
            P(None, "pipe", "head"),
            P(None, None, "head"),
            P(),
            P(),
            P(),
            P("head", None),
            P(("pipe", "head"), None),
            P(),
        ),
        out_specs=P(("pipe", "head"), None),
        check_vma=False,
    )
```

time: 384 us -> 67.6 us (0.18)
  waiting for transfers between devices: 275 us -> 0 us
  Pallas kernels: 0 us -> 65.2 us
  local copies, waits for them, and re-layouts: 50.5 us -> 1.54 us
  matrix products: 20.9 us -> 0 us
  between operations: 14.2 us -> 0.66 us
  starting transfers between devices: 10.2 us -> 0 us
  other arithmetic: 9.15 us -> 0 us
    all_gather x1 -> x0, waiting for transfers between devices: 235 us -> none  [on_device(): whole = lax.all_gather(stale_kv, 'pipe', axis=1, tiled=True)]
    pallas_call x0 -> x1, Pallas kernels: none -> 65.2 us  [on_device(): pl.pallas_call(kernel, out_shape=jax.ShapeDtypeStruct((TOK, D), BF), in_s...]
    reduce_scatter x1 -> x0, waiting for transfers between devices: 34.5 us -> none  [on_device(): lax.psum_scatter(jnp.dot(attn, out_weight, preferred_element_type=jnp.flo...]
    slice x9 -> x0, local copies, waits for them, and re-layouts: 21.7 us -> none  [the longest x8 19.7 us: fold_piece(): piece[1].reshape(count, heads_dev, HEAD_DIM)]
    dot_general x21 -> x0, matrix products: 20.9 us -> none  [the longest x10 14.5 us: attend(): jnp.einsum('hqd,khd->hqk', queries, keys, preferred_element_type=jnp.floa...]
    while x25 -> x0, local copies, waits for them, and re-layouts: 20.7 us -> none
    all_to_all x1 -> x0, starting transfers between devices: 10.2 us -> none  [on_device(): lax.all_to_all(split, 'head', split_axis=2, concat_axis=0, tiled=True)]
    all_to_all x1 -> x0, waiting for transfers between devices: 5.36 us -> none  [on_device(): lax.all_to_all(split, 'head', split_axis=2, concat_axis=0, tiled=True)]
  transfers between devices with their start and end apart: 3 -> 0, of which waited for: 3 -> 0; matrix products, arithmetic and copies ran while one was open for 2% -> 0% of each run, Pallas kernels for 0% -> 0%
where the time goes in v1:
time: 67.6 us; the launch traced here: 67.4 us
  Pallas kernels  65.2 us (96%)
  local copies, waits for them, and re-layouts  1.54 us (2%)
    pallas_call x1, Pallas kernels, on_device(): pl.pallas_call(kernel, out_shape=jax.ShapeDtypeStruct((TOK, D), BF), in_s...  65.2 us
    unnamed x1, local copies, waits for them, and re-layouts  1.54 us

profile of v1, /device:TPU:1, one launch (start us, length us, event | category | flops | bytes accessed | tf_op | source)
XLA Modules:
  0.0 67.4 jit_solution(13965875594455757261)
XLA Ops:
  0.7 65.2 %joint_attention.1 = bf16[16,3072]{1,0:T(8,128)(2,1)} custom-call(bf16[16,9216]{1,0:T(8,128)(2,1)} %fresh.1, bf16[2,128,384]{2,1,0:T(8,128)(2,1)} %stale.1, bf16[2,512,384]{2,1,0:T(8,128)(2,1)} %text.1, s32[1]{0:T(128)S(6)} %copy.11.tlen, f32[1,128]{1,0:T(1,128)} %bitcast.4, f32[1,128]{1,0:T(1,128)} %bitcast.5, bf16[384,3072]{1,0:T(8,128)(2,1)} %w.1, ...), custom_call_target="tpu_custom_call" | custom-call | flops 2000000000 | bytes 4000000 | tf_op jit(solution)/shard_map/joint_attention/pallas_call | solution.py:335
  65.9 1.5 %copy.12 = bf16[16,3072]{1,0:T(8,128)(2,1)} copy(bf16[16,3072]{1,0:T(8,128)(2,1)} %joint_attention.1) | data formatting | bytes 196608

commit v2 on v1

v2 whole, which is shorter than its diff:
```python
import math

import jax
import jax.numpy as jnp
from jax import lax
from jax.experimental import pallas as pl
from jax.experimental.pallas import tpu as pltpu
from jax.sharding import PartitionSpec as P

MESH = pl.DeviceIdType.MESH
HD = 128
HEADS = 3
W = HEADS * HD
PATCH = 128
NX, NZ, NY, NL, NC = 4, 2, 8, 4, 2
NH = NL * NC
HALF = PATCH // 2
TOK = PATCH // NH
OWN = NY
D = 3072
CHUNKS = 3
CW = D // CHUNKS
BF, F32 = jnp.bfloat16, jnp.float32


def dot_nt(a, b):
    return lax.dot_general(a, b, (((1,), (1,)), ((), ())), preferred_element_type=F32)


def spread_rows(column):
    return jnp.transpose(jnp.broadcast_to(column, (PATCH, HD)))[0:8]


def split_three(rows):
    hi = rows.astype(BF).astype(F32)
    rest = rows - hi
    mid = rest.astype(BF).astype(F32)
    low = rest - mid
    at = lax.broadcasted_iota(jnp.int32, rows.shape, 0)
    return jnp.where(at == 0, hi, jnp.where(at == 1, mid, jnp.where(at == 2, low, 0.0)))


def merge(parts, logs):
    top = logs[0]
    for row in logs[1:]:
        top = jnp.maximum(top, row)
    shares = [jnp.exp2(row - top) for row in logs]
    total = shares[0]
    for share in shares[1:]:
        total = total + share
    inverse = 1.0 / total
    at = lax.broadcasted_iota(jnp.int32, (8, HD), 0)
    packed = jnp.zeros((8, HD), F32)
    for i, share in enumerate(shares):
        packed = jnp.where(at == i, share * inverse, packed)
    columns = jnp.transpose(jnp.concatenate([packed] * (PATCH // 8), axis=0))[: parts[0].shape[0]]
    out = columns[:, 0:1] * parts[0]
    for i in range(1, len(parts)):
        out = out + columns[:, i : i + 1] * parts[i]
    return out, top + jnp.log2(total)


def kernel(
    fresh, stale, text, tlen, qg_in, kg_in, w, hidden_in, gate_in, o_ref,
    qraw, kvraw, qall, kv, txt, obuf, orecv, zown, zlog, zsend, zrecv, attn, wv, psend, pown, precv, pfin, rsend, rrecv,
    qg, kg, hidden, gate,
    loc_sem, q_ssem, q_rsem, f_ssem, f_rsem, kv_ssem, kv_rsem, x_ssem, x_rsem, o_ssem, o_rsem, z_ssem, z_rsem,
    p_ssem, p_rsem, r_ssem, r_rsem,
):
    pipe, me = lax.axis_index("pipe"), lax.axis_index("head")
    x, zh, y = pipe // (NZ * NY), (pipe // NY) % NZ, pipe % NY
    zl, core = me // NC, me % NC

    def at_x(j):
        return ((((x + j) % NX) * NZ + zh) * NY + y, me)

    def at_y(j):
        return ((x * NZ + zh) * NY + (y + j) % NY, me)

    def at_head(r, i):
        return ((x * NZ + (zh + r) % NZ) * NY + y, (me + i) % NH)

    pair = (pipe, zl * NC + 1 - core)

    def remote(src, dst, ssem, rsem, dev):
        return pltpu.make_async_remote_copy(
            src_ref=src, dst_ref=dst, send_sem=ssem, recv_sem=rsem, device_id=dev, device_id_type=MESH
        )

    bar = pltpu.get_barrier_semaphore()
    partners = [at_x(j) for j in range(1, NX)] + [at_y(1), at_y(NY - 1)]
    partners += [at_head(r, i) for r in range(NZ) for i in range(NH) if (r, i) != (0, 0)]
    for dev in partners:
        pl.semaphore_signal(bar, inc=1, device_id=dev, device_id_type=MESH)

    share = x * NZ + zh
    get_w = pltpu.make_async_copy(w, wv, loc_sem.at[0])
    get_text = pltpu.make_async_copy(
        text.at[:, pl.ds(pl.multiple_of((share // 2) * 128, 128), 128), :], txt, loc_sem.at[1]
    )
    get_small = [
        pltpu.make_async_copy(src, dst, loc_sem.at[2 + n])
        for n, (src, dst) in enumerate(((qg_in, qg), (kg_in, kg), (hidden_in, hidden), (gate_in, gate)))
    ]
    get_own = [
        pltpu.make_async_copy(stale.at[:, :, pl.ds(h * HD, HD)], kv.at[h, OWN], loc_sem.at[6 + h])
        for h in range(HEADS)
    ]

    def head_cols(part, i):
        return fresh.at[:, pl.ds(pl.multiple_of(part * D + ((me + i) % NH) * W, W), W)]

    my_half, my_spot = ((zl + 1) // 2) % 2, (zl // 2) * NC + core

    def q_hop(r, i):
        return remote(
            head_cols(0, i), qraw.at[my_half, r, my_spot], q_ssem.at[r, i], q_rsem.at[r, i], at_head(r, i)
        )

    def f_hop(part, i):
        return remote(head_cols(part + 1, i), kvraw.at[part, i], f_ssem.at[part, i], f_rsem.at[part, i], at_head(0, i))

    q_local = pltpu.make_async_copy(head_cols(0, 0), qraw.at[my_half, 0, my_spot], q_rsem.at[0, 0])
    f_local = [
        pltpu.make_async_copy(head_cols(part + 1, 0), kvraw.at[part, 0], f_rsem.at[part, 0]) for part in range(2)
    ]
    q_local.start()
    for copy in get_small[:2]:
        copy.start()
    pl.semaphore_wait(bar, len(partners))

    for r in (1, 0):
        for i in range(NH):
            if (r, i) != (0, 0):
                q_hop(r, i).start()

    def hop(h, slot):
        if slot == 1 or slot == NY - 1:
            src = stale.at[:, :, pl.ds(h * HD, HD)]
        elif slot == 40:
            src = kv.at[h, 3, 0]
        elif slot == 41:
            src = kv.at[h, 5, 1]
        else:
            src = kv.at[h, slot - 1 if slot < 4 else slot + 1]
        if slot >= 40:
            dst = kv.at[h, 4, slot - 40]
        else:
            dst = kv.at[h, slot]
        sem = {40: 0, 41: 4}.get(slot, slot)
        up = slot < 4 or slot == 40
        return remote(src, dst, kv_ssem.at[h, sem], kv_rsem.at[h, sem], at_y(1 if up else NY - 1))

    for h in range(HEADS):
        hop(h, 1).start()
        hop(h, 7).start()

    for copy in [*get_own, get_text, get_w, *get_small[2:]]:
        copy.start()

    for part in range(2):
        f_local[part].start()
        for i in range(1, NH):
            f_hop(part, i).start()

    for h in range(HEADS):
        hop(h, 1).wait_recv()
        hop(h, 2).start()
        hop(h, 7).wait_recv()
        hop(h, 6).start()

    scale = math.log2(math.e) / math.sqrt(HD)

    def normed(rows, gain):
        return (rows * lax.rsqrt(jnp.mean(rows * rows, axis=-1, keepdims=True) + 1e-06) * gain[...]).astype(BF)

    def x_hop(half, j):
        return remote(
            qall.at[half, 0], qall.at[half, NX - j], x_ssem.at[half, j], x_rsem.at[half, NX - j], at_x(j)
        )

    for copy in get_small[:2]:
        copy.wait()
    q_local.wait()
    for r in range(NZ):
        for i in range(NH):
            if (r, i) != (0, 0):
                q_hop(r, i).wait_recv()
    for half in range(2):
        for h in range(HEADS):
            rows = qraw[half, :, :, :, pl.ds(h * HD, HD)].reshape(PATCH, HD).astype(F32)
            qall[half, 0, h] = normed(rows, qg)
        for j in (2, 1, 3):
            x_hop(half, j).start()

    for h in range(HEADS):
        hop(h, 2).wait_recv()
        hop(h, 3).start()
        hop(h, 6).wait_recv()
        hop(h, 5).start()

    for part in range(2):
        f_local[part].wait()
        for i in range(1, NH):
            f_hop(part, i).wait_recv()
    for h in range(HEADS):
        cols = pl.ds(h * HD, HD)
        kv[h, 0, 0] = normed(kvraw[0, :, :, cols].reshape(PATCH, HD).astype(F32), kg)
        kv[h, 0, 1] = kvraw[1, :, :, cols].reshape(PATCH, HD)

    for h in range(HEADS):
        hop(h, 3).wait_recv()
        hop(h, 40).start()
        hop(h, 5).wait_recv()
        hop(h, 41).start()

    for copy in get_own:
        copy.wait()
    get_text.wait()
    spot = lax.broadcasted_iota(jnp.int32, (1, 128), 1)
    live = (spot // 64 == share % 2) & (spot + (share // 2) * 128 < tlen[0])
    bias = jnp.where(live, 0.0, -1e30)

    def o_hop(half, j):
        return remote(
            obuf.at[half, j], orecv.at[half, NX - j], o_ssem.at[half, j], o_rsem.at[half, NX - j], at_x(j)
        )

    def z_hop(half):
        return remote(zsend.at[half], zrecv.at[half], z_ssem.at[half], z_rsem.at[half], at_head(1, 0))

    def soft(q, h, first):
        slots = pl.ds(first, NY)
        scores = dot_nt(q, kv[h, slots, 0].reshape(NY * PATCH, HD))
        tscores = dot_nt(q, txt[0, :, pl.ds(h * HD, HD)]) + bias
        top = jnp.maximum(jnp.max(scores, axis=-1, keepdims=True), jnp.max(tscores, axis=-1, keepdims=True))
        e, te = jnp.exp2((scores - top) * scale), jnp.exp2((tscores - top) * scale)
        total = jnp.sum(e, axis=-1, keepdims=True) + jnp.sum(te, axis=-1, keepdims=True)
        out = jnp.dot(e.astype(BF), kv[h, slots, 1].reshape(NY * PATCH, HD), preferred_element_type=F32)
        out = out + jnp.dot(te.astype(BF), txt[1, :, pl.ds(h * HD, HD)], preferred_element_type=F32)
        return out * (1.0 / total), top * scale + jnp.log2(total)

    def attend(half, j):
        for h in range(HEADS):
            if j == 0:
                two = [soft(qall[half, 0, h, pl.ds(r * HALF, HALF), :], h, r) for r in range(NZ)]
                out, log = (jnp.concatenate([a, b], axis=0) for a, b in zip(*two))
            else:
                out, log = soft(qall[half, j, h], h, 1)
            obuf[half, j, h, pl.ds(0, PATCH), :] = out.astype(BF)
            obuf[half, j, h, pl.ds(PATCH, 16), :] = packed(spread_rows(log))
        if j > 0:
            o_hop(half, j).start()

    def packed(rows):
        return jnp.concatenate([split_three(rows), jnp.zeros((8, HD), F32)], axis=0).astype(BF)

    def logs_of(rows):
        rows = rows.astype(F32)
        return rows[0:1] + rows[1:2] + rows[2:3]

    def merge_x(half):
        for j in range(1, NX):
            o_hop(half, j).wait_recv()
        for h in range(HEADS):
            sources = [obuf.at[half, 0, h]] + [orecv.at[half, j, h] for j in range(1, NX)]
            parts = [s[pl.ds(0, PATCH), :].astype(F32) for s in sources]
            out, log = merge(parts, [logs_of(s[pl.ds(PATCH, 16), :]) for s in sources])
            log = jnp.broadcast_to(log, (8, HD))
            zsend[half, h, pl.ds(0, HALF), :] = out[HALF:].astype(BF)
            zsend[half, h, pl.ds(HALF, 16), :] = packed(pltpu.roll(log, HALF, 1))
            zown[half, h] = out[:HALF]
            zlog[half, h] = log
        z_hop(half).start()

    def merge_z(half):
        z_hop(half).wait_recv()
        for h in range(HEADS):
            out, _ = merge(
                [zown[half, h], zrecv[half, h, pl.ds(0, HALF), :].astype(F32)],
                [zlog[half, h, 0:1], logs_of(zrecv[half, h, pl.ds(HALF, 16), :])],
            )
            attn[half, :, :, pl.ds(h * HD, HD)] = out.astype(BF).reshape(NH // 2, TOK, HD)

    def p_hop(half, c):
        return remote(psend.at[half, c], precv.at[half, c], p_ssem.at[half, c], p_rsem.at[half, c], pair)

    def project(half):
        rows = jnp.concatenate([attn[half, n * NC + c] for c in (1 - core, core) for n in range(2)], axis=0)
        for c in range(CHUNKS):
            part = jnp.dot(rows, wv[:, pl.ds(c * CW, CW)], preferred_element_type=F32)
            psend[half, c] = part[: 2 * TOK].astype(BF)
            p_hop(half, c).start()
            pown[half, c] = part[2 * TOK :]

    def r_hop(half, c, n):
        owner = ((0, 3), (1, 2))[half][n]
        away = (owner + NL - zl) % NL
        return remote(
            rsend.at[half, c, n], rrecv.at[c, away], r_ssem.at[half, c, n], r_rsem.at[c, away], (pipe, owner * NC + core)
        )

    def arrived(c, away):
        return remote(rsend.at[0, c, 0], rrecv.at[c, away], r_ssem.at[0, c, 0], r_rsem.at[c, away], pair)

    def reduce(half):
        for c in range(CHUNKS):
            p_hop(half, c).wait_recv()
            both = pown[half, c] + precv[half, c].astype(F32)
            for n in range(2):
                owner = ((0, 3), (1, 2))[half][n]
                mine = both[n * TOK : (n + 1) * TOK]
                rsend[half, c, n] = mine.astype(BF)

                @pl.when(zl != owner)
                def _():
                    r_hop(half, c, n).start()

                @pl.when(zl == owner)
                def _():
                    pfin[c] = mine

    for half in range(2):
        for j in range(1, NX):
            x_hop(half, j).wait_recv()
        if half == 0:
            for h in range(HEADS):
                hop(h, 40).wait_recv()
                hop(h, 41).wait_recv()
        for j in (2, 1, 3):
            attend(half, j)
        if half == 1:
            merge_x(0)
        attend(half, 0)
    merge_x(1)
    merge_z(0)
    get_w.wait()
    project(0)
    reduce(0)
    merge_z(1)
    project(1)
    reduce(1)

    for copy in get_small[2:]:
        copy.wait()
    for c in range(CHUNKS):
        cols = pl.ds(c * CW, CW)
        for i in range(1, NL):
            arrived(c, i).wait_recv()
        total = pfin[c]
        for i in range(1, NL):
            total = total + rrecv[c, i].astype(F32)
        o_ref[:, cols] = (hidden[:, cols].astype(F32) + gate[:, cols] * total).astype(BF)

    for r in range(2):
        for i in range(NH):
            if (r, i) != (0, 0):
                q_hop(r, i).wait_send()
            if i > 0:
                f_hop(r, i).wait_send()
    for h in range(HEADS):
        for slot in (1, 2, 3, 40, 41, 5, 6, 7):
            hop(h, slot).wait_send()
    for half in range(2):
        for j in range(1, NX):
            x_hop(half, j).wait_send()
            o_hop(half, j).wait_send()
        z_hop(half).wait_send()
        for c in range(CHUNKS):
            p_hop(half, c).wait_send()
            for n in range(2):

                @pl.when(zl != ((0, 3), (1, 2))[half][n])
                def _():
                    r_hop(half, c, n).wait_send()


def on_device(fresh, stale, text, tlen, qg, kg, w, hidden, gate):
    dma = pltpu.SemaphoreType.DMA
    hbm, vmem = pl.BlockSpec(memory_space=pl.ANY), pl.BlockSpec(memory_space=pltpu.VMEM)
    return pl.pallas_call(
        kernel,
        out_shape=jax.ShapeDtypeStruct((TOK, D), BF),
        in_specs=[hbm, hbm, hbm, pl.BlockSpec(memory_space=pltpu.SMEM), hbm, hbm, hbm, hbm, hbm],
        out_specs=vmem,
        scratch_shapes=[
            pltpu.VMEM((2, NZ, NH // 2, TOK, W), BF),
            pltpu.VMEM((2, NH, TOK, W), BF),
            pltpu.VMEM((2, NX, HEADS, PATCH, HD), BF),
            pltpu.VMEM((HEADS, NY + 1, 2, PATCH, HD), BF),
            pltpu.VMEM((2, 128, W), BF),
            pltpu.VMEM((2, NX, HEADS, PATCH + 16, HD), BF),
            pltpu.VMEM((2, NX, HEADS, PATCH + 16, HD), BF),
            pltpu.VMEM((2, HEADS, HALF, HD), F32),
            pltpu.VMEM((2, HEADS, 8, HD), F32),
            pltpu.VMEM((2, HEADS, HALF + 16, HD), BF),
            pltpu.VMEM((2, HEADS, HALF + 16, HD), BF),
            pltpu.VMEM((2, NH // 2, TOK, W), BF),
            pltpu.VMEM((W, D), BF),
            pltpu.VMEM((2, CHUNKS, 2 * TOK, CW), BF),
            pltpu.VMEM((2, CHUNKS, 2 * TOK, CW), F32),
            pltpu.VMEM((2, CHUNKS, 2 * TOK, CW), BF),
            pltpu.VMEM((CHUNKS, TOK, CW), F32),
            pltpu.VMEM((2, CHUNKS, 2, TOK, CW), BF),
            pltpu.VMEM((CHUNKS, NL, TOK, CW), BF),
            pltpu.VMEM((1, HD), F32),
            pltpu.VMEM((1, HD), F32),
            pltpu.VMEM((TOK, D), BF),
            pltpu.VMEM((1, D), F32),
            dma((6 + HEADS,)), dma((NZ, NH)), dma((NZ, NH)), dma((2, NH)), dma((2, NH)), dma((HEADS, NY)),
            dma((HEADS, NY)), dma((2, NX)), dma((2, NX)), dma((2, NX)), dma((2, NX)), dma((2,)), dma((2,)),
            dma((2, CHUNKS)), dma((2, CHUNKS)), dma((2, CHUNKS, 2)), dma((CHUNKS, NL)),
        ],
        name="joint_attention",
        cost_estimate=pl.CostEstimate(flops=2 * 10**9, bytes_accessed=4 * 10**6, transcendentals=4 * 10**6),
        compiler_params=pltpu.CompilerParams(
            collective_id=0, has_side_effects=True, vmem_limit_bytes=60 * 2**20
        ),
    )(fresh, stale, text, tlen, qg.reshape(1, HD), kg.reshape(1, HD), w, hidden, gate.reshape(1, D))


def solution(mesh):
    return jax.shard_map(
        on_device,
        mesh=mesh,
        in_specs=(
            P(("pipe", "head"), None),
            P(None, "pipe", "head"),
            P(None, None, "head"),
            P(),
            P(),
            P(),
            P("head", None),
            P(("pipe", "head"), None),
            P(),
        ),
        out_specs=P(("pipe", "head"), None),
        check_vma=False,
    )
```

time: 67.6 us -> 64.4 us (0.953)
  Pallas kernels: 65.2 us -> 61.8 us
    pallas_call x1, Pallas kernels: 65.2 us -> 61.8 us  [on_device(): pl.pallas_call(kernel, out_shape=jax.ShapeDtypeStruct((TOK, D), BF), in_s...]
where the time goes in v2:
time: 64.4 us; the launch traced here: 64 us
  Pallas kernels  61.8 us (96%)
  local copies, waits for them, and re-layouts  1.54 us (2%)
  between operations  0.66 us (1%)
    pallas_call x1, Pallas kernels, on_device(): pl.pallas_call(kernel, out_shape=jax.ShapeDtypeStruct((TOK, D), BF), in_s...  61.8 us
    unnamed x1, local copies, waits for them, and re-layouts  1.54 us

profile of v2, /device:TPU:1, one launch (start us, length us, event | category | flops | bytes accessed | tf_op | source)
XLA Modules:
  0.0 64.0 jit_solution(3155373566483183557)
XLA Ops:
  0.7 61.8 %joint_attention.1 = bf16[16,3072]{1,0:T(8,128)(2,1)} custom-call(bf16[16,9216]{1,0:T(8,128)(2,1)} %fresh.1, bf16[2,128,384]{2,1,0:T(8,128)(2,1)} %stale.1, bf16[2,512,384]{2,1,0:T(8,128)(2,1)} %text.1, s32[1]{0:T(128)S(6)} %copy.11.tlen, f32[1,128]{1,0:T(1,128)} %bitcast.4, f32[1,128]{1,0:T(1,128)} %bitcast.5, bf16[384,3072]{1,0:T(8,128)(2,1)} %w.1, ...), custom_call_target="tpu_custom_call" | custom-call | flops 2000000000 | bytes 4000000 | tf_op jit(solution)/shard_map/joint_attention/pallas_call | solution.py:381
  62.4 1.5 %copy.12 = bf16[16,3072]{1,0:T(8,128)(2,1)} copy(bf16[16,3072]{1,0:T(8,128)(2,1)} %joint_attention.1) | data formatting | bytes 196608

commit v3 on v2

--- a/solution.py
+++ b/solution.py
@@ -16,7 +16,8 @@
 NH = NL * NC
 HALF = PATCH // 2
 TOK = PATCH // NH
-OWN = NY
+OWN, TEXT, NEW = 0, NY, NY + 1
+STAT = 32
 D = 3072
 CHUNKS = 3
 CW = D // CHUNKS
@@ -27,42 +28,45 @@
     return lax.dot_general(a, b, (((1,), (1,)), ((), ())), preferred_element_type=F32)
 
 
-def spread_rows(column):
-    return jnp.transpose(jnp.broadcast_to(column, (PATCH, HD)))[0:8]
-
-
-def split_three(rows):
+def three_parts(rows):
     hi = rows.astype(BF).astype(F32)
-    rest = rows - hi
-    mid = rest.astype(BF).astype(F32)
-    low = rest - mid
-    at = lax.broadcasted_iota(jnp.int32, rows.shape, 0)
-    return jnp.where(at == 0, hi, jnp.where(at == 1, mid, jnp.where(at == 2, low, 0.0)))
-
-
-def merge(parts, logs):
-    top = logs[0]
-    for row in logs[1:]:
+    mid = (rows - hi).astype(BF).astype(F32)
+    return jnp.concatenate([hi, mid, rows - hi - mid, jnp.zeros_like(rows)], axis=0).astype(BF)
+
+
+def whole(parts):
+    parts = parts.astype(F32)
+    return parts[0:8] + parts[8:16] + parts[16:24]
+
+
+def with_ones(values):
+    return jnp.concatenate([values, jnp.ones_like(values)], axis=1)
+
+
+def shares(stats):
+    top = stats[0][0]
+    for row, _ in stats[1:]:
         top = jnp.maximum(top, row)
-    shares = [jnp.exp2(row - top) for row in logs]
-    total = shares[0]
-    for share in shares[1:]:
-        total = total + share
-    inverse = 1.0 / total
-    at = lax.broadcasted_iota(jnp.int32, (8, HD), 0)
-    packed = jnp.zeros((8, HD), F32)
-    for i, share in enumerate(shares):
-        packed = jnp.where(at == i, share * inverse, packed)
-    columns = jnp.transpose(jnp.concatenate([packed] * (PATCH // 8), axis=0))[: parts[0].shape[0]]
-    out = columns[:, 0:1] * parts[0]
-    for i in range(1, len(parts)):
-        out = out + columns[:, i : i + 1] * parts[i]
-    return out, top + jnp.log2(total)
+    factors = [jnp.exp2(row - top) for row, _ in stats]
+    total = factors[0] * stats[0][1]
+    for factor, (_, part) in zip(factors[1:], stats[1:]):
+        total = total + factor * part
+    return top, factors, total
+
+
+def diagonal(row, first):
+    shape = (HALF, HD)
+    on = lax.broadcasted_iota(jnp.int32, shape, 0) + first == lax.broadcasted_iota(jnp.int32, shape, 1)
+    return jnp.where(on, row, 0.0).astype(BF)
+
+
+def dot(a, b):
+    return jnp.dot(a, b, preferred_element_type=F32)
 
 
 def kernel(
     fresh, stale, text, tlen, qg_in, kg_in, w, hidden_in, gate_in, o_ref,
-    qraw, kvraw, qall, kv, txt, obuf, orecv, zown, zlog, zsend, zrecv, attn, wv, psend, pown, precv, pfin, rsend, rrecv,
+    qraw, kvraw, qall, kv, obuf, orecv, zsend, zrecv, attn, wv, psend, pown, precv, pfin, rsend, rrecv,
     qg, kg, hidden, gate,
     loc_sem, q_ssem, q_rsem, f_ssem, f_rsem, kv_ssem, kv_rsem, x_ssem, x_rsem, o_ssem, o_rsem, z_ssem, z_rsem,
     p_ssem, p_rsem, r_ssem, r_rsem,
@@ -95,9 +99,11 @@
 
     share = x * NZ + zh
     get_w = pltpu.make_async_copy(w, wv, loc_sem.at[0])
-    get_text = pltpu.make_async_copy(
-        text.at[:, pl.ds(pl.multiple_of((share // 2) * 128, 128), 128), :], txt, loc_sem.at[1]
-    )
+    window = pl.ds(pl.multiple_of((share // 2) * 128, 128), 128)
+    get_text = [
+        pltpu.make_async_copy(text.at[:, window, pl.ds(h * HD, HD)], kv.at[h, TEXT], loc_sem.at[6 + HEADS + h])
+        for h in range(HEADS)
+    ]
     get_small = [
         pltpu.make_async_copy(src, dst, loc_sem.at[2 + n])
         for n, (src, dst) in enumerate(((qg_in, qg), (kg_in, kg), (hidden_in, hidden), (gate_in, gate)))
@@ -155,7 +161,7 @@
         hop(h, 1).start()
         hop(h, 7).start()
 
-    for copy in [*get_own, get_text, get_w, *get_small[2:]]:
+    for copy in [*get_own, *get_text, get_w, *get_small[2:]]:
         copy.start()
 
     for part in range(2):
@@ -205,8 +211,8 @@
             f_hop(part, i).wait_recv()
     for h in range(HEADS):
         cols = pl.ds(h * HD, HD)
-        kv[h, 0, 0] = normed(kvraw[0, :, :, cols].reshape(PATCH, HD).astype(F32), kg)
-        kv[h, 0, 1] = kvraw[1, :, :, cols].reshape(PATCH, HD)
+        kv[h, NEW, 0] = normed(kvraw[0, :, :, cols].reshape(PATCH, HD).astype(F32), kg)
+        kv[h, NEW, 1] = kvraw[1, :, :, cols].reshape(PATCH, HD)
 
     for h in range(HEADS):
         hop(h, 3).wait_recv()
@@ -214,72 +220,77 @@
         hop(h, 5).wait_recv()
         hop(h, 41).start()
 
-    for copy in get_own:
+    for copy in get_own + get_text:
         copy.wait()
-    get_text.wait()
     spot = lax.broadcasted_iota(jnp.int32, (1, 128), 1)
     live = (spot // 64 == share % 2) & (spot + (share // 2) * 128 < tlen[0])
     bias = jnp.where(live, 0.0, -1e30)
 
-    def o_hop(half, j):
+    def o_hop(half, h, j):
         return remote(
-            obuf.at[half, j], orecv.at[half, NX - j], o_ssem.at[half, j], o_rsem.at[half, NX - j], at_x(j)
+            obuf.at[half, h, j], orecv.at[half, h, NX - j], o_ssem.at[half, h, j], o_rsem.at[half, h, NX - j], at_x(j)
         )
 
     def z_hop(half):
         return remote(zsend.at[half], zrecv.at[half], z_ssem.at[half], z_rsem.at[half], at_head(1, 0))
 
-    def soft(q, h, first):
-        slots = pl.ds(first, NY)
-        scores = dot_nt(q, kv[h, slots, 0].reshape(NY * PATCH, HD))
-        tscores = dot_nt(q, txt[0, :, pl.ds(h * HD, HD)]) + bias
-        top = jnp.maximum(jnp.max(scores, axis=-1, keepdims=True), jnp.max(tscores, axis=-1, keepdims=True))
-        e, te = jnp.exp2((scores - top) * scale), jnp.exp2((tscores - top) * scale)
-        total = jnp.sum(e, axis=-1, keepdims=True) + jnp.sum(te, axis=-1, keepdims=True)
-        out = jnp.dot(e.astype(BF), kv[h, slots, 1].reshape(NY * PATCH, HD), preferred_element_type=F32)
-        out = out + jnp.dot(te.astype(BF), txt[1, :, pl.ds(h * HD, HD)], preferred_element_type=F32)
-        return out * (1.0 / total), top * scale + jnp.log2(total)
-
-    def attend(half, j):
+    def attend(half, h):
+        q = qall[half, :, h].reshape(NX * PATCH, HD)
+        keys = kv[h, pl.ds(1, NY), 0].reshape(NY * PATCH, HD)
+        values = kv[h, pl.ds(1, NY), 1].reshape(NY * PATCH, HD)
+        scores = dot_nt(q, keys)
+        split = (NY - 1) * PATCH
+        scores = jnp.concatenate([scores[:, :split], scores[:, split:] + bias], axis=1)
+        mine = jnp.concatenate([dot_nt(q[:HALF], kv[h, NEW, 0]), dot_nt(q[HALF:], kv[h, OWN, 0])], axis=0)
+        top = jnp.maximum(jnp.max(scores, axis=-1, keepdims=True), jnp.max(mine, axis=-1, keepdims=True))
+        e = jnp.exp2((scores - top) * scale).astype(BF)
+        e_mine = jnp.exp2((mine - top) * scale).astype(BF)
+        own = [dot(e_mine[:HALF], with_ones(kv[h, NEW, 1])), dot(e_mine[HALF:], with_ones(kv[h, OWN, 1]))]
+        out = dot(e, with_ones(values)) + jnp.concatenate(own, axis=0)
+        top = top * scale
+        lane = lax.broadcasted_iota(jnp.int32, (PATCH, HD), 1)
+        table = jnp.zeros((PATCH, HD), F32)
+        for j in range(NX):
+            rows = slice(j * PATCH, (j + 1) * PATCH)
+            obuf[half, h, j, pl.ds(0, PATCH), :] = out[rows, :HD].astype(BF)
+            table = jnp.where(lane == j, top[rows], jnp.where(lane == NX + j, out[rows, HD:], table))
+        stats = three_parts(jnp.transpose(table)[0:8])
+        for j in range(NX):
+            obuf[half, h, j, pl.ds(PATCH, STAT), :] = stats
+        for j in (2, 1, 3):
+            o_hop(half, h, j).start()
+
+    def sources(half, h):
+        refs = [obuf.at[half, h, 0]] + [orecv.at[half, h, j] for j in range(1, NX)]
+        stats = []
+        for j, ref in enumerate(refs):
+            rows, at = whole(ref[pl.ds(PATCH, STAT), :]), (NX - j) % NX
+            stats.append((rows[at : at + 1], rows[NX + at : NX + at + 1]))
+        return jnp.concatenate([ref[pl.ds(0, PATCH), :] for ref in refs], axis=0), stats
+
+    def merge_x(half):
         for h in range(HEADS):
-            if j == 0:
-                two = [soft(qall[half, 0, h, pl.ds(r * HALF, HALF), :], h, r) for r in range(NZ)]
-                out, log = (jnp.concatenate([a, b], axis=0) for a, b in zip(*two))
-            else:
-                out, log = soft(qall[half, j, h], h, 1)
-            obuf[half, j, h, pl.ds(0, PATCH), :] = out.astype(BF)
-            obuf[half, j, h, pl.ds(PATCH, 16), :] = packed(spread_rows(log))
-        if j > 0:
-            o_hop(half, j).start()
-
-    def packed(rows):
-        return jnp.concatenate([split_three(rows), jnp.zeros((8, HD), F32)], axis=0).astype(BF)
-
-    def logs_of(rows):
-        rows = rows.astype(F32)
-        return rows[0:1] + rows[1:2] + rows[2:3]
-
-    def merge_x(half):
-        for j in range(1, NX):
-            o_hop(half, j).wait_recv()
-        for h in range(HEADS):
-            sources = [obuf.at[half, 0, h]] + [orecv.at[half, j, h] for j in range(1, NX)]
-            parts = [s[pl.ds(0, PATCH), :].astype(F32) for s in sources]
-            out, log = merge(parts, [logs_of(s[pl.ds(PATCH, 16), :]) for s in sources])
-            log = jnp.broadcast_to(log, (8, HD))
-            zsend[half, h, pl.ds(0, HALF), :] = out[HALF:].astype(BF)
-            zsend[half, h, pl.ds(HALF, 16), :] = packed(pltpu.roll(log, HALF, 1))
-            zown[half, h] = out[:HALF]
-            zlog[half, h] = log
+            for j in range(1, NX):
+                o_hop(half, h, j).wait_recv()
+            parts, stats = sources(half, h)
+            top, factors, total = shares(stats)
+            out = dot(jnp.concatenate([diagonal(f, HALF) for f in factors], axis=1), parts)
+            zsend[half, h, pl.ds(0, HALF), :] = out.astype(BF)
+            row = lax.broadcasted_iota(jnp.int32, (8, HD), 0)
+            table = jnp.where(row == 0, top, jnp.where(row == 1, total, 0.0))
+            zsend[half, h, pl.ds(HALF, STAT), :] = three_parts(pltpu.roll(table, HALF, 1))
         z_hop(half).start()
 
     def merge_z(half):
         z_hop(half).wait_recv()
         for h in range(HEADS):
-            out, _ = merge(
-                [zown[half, h], zrecv[half, h, pl.ds(0, HALF), :].astype(F32)],
-                [zlog[half, h, 0:1], logs_of(zrecv[half, h, pl.ds(HALF, 16), :])],
-            )
+            parts, stats = sources(half, h)
+            far = whole(zrecv[half, h, pl.ds(HALF, STAT), :])
+            _, factors, total = shares(stats + [(far[0:1], far[1:2])])
+            inverse = 1.0 / total
+            weights = [diagonal(f * inverse, 0) for f in factors]
+            out = dot(jnp.concatenate(weights[:NX], axis=1), parts)
+            out = out + dot(weights[NX][:, :HALF], zrecv[half, h, pl.ds(0, HALF), :])
             attn[half, :, :, pl.ds(h * HD, HD)] = out.astype(BF).reshape(NH // 2, TOK, HD)
 
     def p_hop(half, c):
@@ -323,15 +334,12 @@
     for half in range(2):
         for j in range(1, NX):
             x_hop(half, j).wait_recv()
-        if half == 0:
-            for h in range(HEADS):
+        for h in range(HEADS):
+            if half == 0:
                 hop(h, 40).wait_recv()
                 hop(h, 41).wait_recv()
-        for j in (2, 1, 3):
-            attend(half, j)
-        if half == 1:
-            merge_x(0)
-        attend(half, 0)
+            attend(half, h)
+    merge_x(0)
     merge_x(1)
     merge_z(0)
     get_w.wait()
@@ -364,7 +372,8 @@
     for half in range(2):
         for j in range(1, NX):
             x_hop(half, j).wait_send()
-            o_hop(half, j).wait_send()
+            for h in range(HEADS):
+                o_hop(half, h, j).wait_send()
         z_hop(half).wait_send()
         for c in range(CHUNKS):
             p_hop(half, c).wait_send()
@@ -387,14 +396,11 @@
             pltpu.VMEM((2, NZ, NH // 2, TOK, W), BF),
             pltpu.VMEM((2, NH, TOK, W), BF),
             pltpu.VMEM((2, NX, HEADS, PATCH, HD), BF),
-            pltpu.VMEM((HEADS, NY + 1, 2, PATCH, HD), BF),
-            pltpu.VMEM((2, 128, W), BF),
-            pltpu.VMEM((2, NX, HEADS, PATCH + 16, HD), BF),
-            pltpu.VMEM((2, NX, HEADS, PATCH + 16, HD), BF),
-            pltpu.VMEM((2, HEADS, HALF, HD), F32),
-            pltpu.VMEM((2, HEADS, 8, HD), F32),
-            pltpu.VMEM((2, HEADS, HALF + 16, HD), BF),
-            pltpu.VMEM((2, HEADS, HALF + 16, HD), BF),
+            pltpu.VMEM((HEADS, NY + 2, 2, PATCH, HD), BF),
+            pltpu.VMEM((2, HEADS, NX, PATCH + STAT, HD), BF),
+            pltpu.VMEM((2, HEADS, NX, PATCH + STAT, HD), BF),
+            pltpu.VMEM((2, HEADS, HALF + STAT, HD), BF),
+            pltpu.VMEM((2, HEADS, HALF + STAT, HD), BF),
             pltpu.VMEM((2, NH // 2, TOK, W), BF),
             pltpu.VMEM((W, D), BF),
             pltpu.VMEM((2, CHUNKS, 2 * TOK, CW), BF),
@@ -407,8 +413,8 @@
             pltpu.VMEM((1, HD), F32),
             pltpu.VMEM((TOK, D), BF),
             pltpu.VMEM((1, D), F32),
-            dma((6 + HEADS,)), dma((NZ, NH)), dma((NZ, NH)), dma((2, NH)), dma((2, NH)), dma((HEADS, NY)),
-            dma((HEADS, NY)), dma((2, NX)), dma((2, NX)), dma((2, NX)), dma((2, NX)), dma((2,)), dma((2,)),
+            dma((6 + 2 * HEADS,)), dma((NZ, NH)), dma((NZ, NH)), dma((2, NH)), dma((2, NH)), dma((HEADS, NY)),
+            dma((HEADS, NY)), dma((2, NX)), dma((2, NX)), dma((2, HEADS, NX)), dma((2, HEADS, NX)), dma((2,)), dma((2,)),
             dma((2, CHUNKS)), dma((2, CHUNKS)), dma((2, CHUNKS, 2)), dma((CHUNKS, NL)),
         ],
         name="joint_attention",

time: 64.4 us -> 62.9 us (0.977)
  Pallas kernels: 61.8 us -> 60.6 us
    pallas_call x1, Pallas kernels: 61.8 us -> 60.6 us  [on_device(): pl.pallas_call(kernel, out_shape=jax.ShapeDtypeStruct((TOK, D), BF), in_s...]
where the time goes in v3:
time: 62.9 us; the launch traced here: 62.8 us
  Pallas kernels  60.6 us (96%)
  local copies, waits for them, and re-layouts  1.54 us (2%)
  between operations  0.66 us (1%)
    pallas_call x1, Pallas kernels, on_device(): pl.pallas_call(kernel, out_shape=jax.ShapeDtypeStruct((TOK, D), BF), in_s...  60.6 us
    unnamed x1, local copies, waits for them, and re-layouts  1.54 us

profile of v3, /device:TPU:1, one launch (start us, length us, event | category | flops | bytes accessed | tf_op | source)
XLA Modules:
  0.0 62.8 jit_solution(5403532614616164106)
XLA Ops:
  0.7 60.6 %joint_attention.1 = bf16[16,3072]{1,0:T(8,128)(2,1)} custom-call(bf16[16,9216]{1,0:T(8,128)(2,1)} %fresh.1, bf16[2,128,384]{2,1,0:T(8,128)(2,1)} %stale.1, bf16[2,512,384]{2,1,0:T(8,128)(2,1)} %text.1, s32[1]{0:T(128)S(6)} %copy.11.tlen, f32[1,128]{1,0:T(1,128)} %bitcast.4, f32[1,128]{1,0:T(1,128)} %bitcast.5, bf16[384,3072]{1,0:T(8,128)(2,1)} %w.1, ...), custom_call_target="tpu_custom_call" | custom-call | flops 2000000000 | bytes 4000000 | tf_op jit(solution)/shard_map/joint_attention/pallas_call | solution.py:390
  61.2 1.5 %copy.12 = bf16[16,3072]{1,0:T(8,128)(2,1)} copy(bf16[16,3072]{1,0:T(8,128)(2,1)} %joint_attention.1) | data formatting | bytes 196608

commit v4 on v3

--- a/solution.py
+++ b/solution.py
@@ -16,7 +16,7 @@
 NH = NL * NC
 HALF = PATCH // 2
 TOK = PATCH // NH
-OWN, TEXT, NEW = 0, NY, NY + 1
+OWN, TEXT, FAR, NEW = 0, 7, 8, 9
 STAT = 32
 D = 3072
 CHUNKS = 3
@@ -141,25 +141,20 @@
                 q_hop(r, i).start()
 
     def hop(h, slot):
-        if slot == 1 or slot == NY - 1:
+        up = slot in (1, 2, 3, 40)
+        if slot in (1, 6):
             src = stale.at[:, :, pl.ds(h * HD, HD)]
-        elif slot == 40:
-            src = kv.at[h, 3, 0]
-        elif slot == 41:
-            src = kv.at[h, 5, 1]
+        elif slot >= 40:
+            src = kv.at[h, 3 if up else 4, slot - 40]
         else:
-            src = kv.at[h, slot - 1 if slot < 4 else slot + 1]
-        if slot >= 40:
-            dst = kv.at[h, 4, slot - 40]
-        else:
-            dst = kv.at[h, slot]
-        sem = {40: 0, 41: 4}.get(slot, slot)
-        up = slot < 4 or slot == 40
+            src = kv.at[h, slot - 1 if up else slot + 1]
+        dst = kv.at[h, FAR, slot - 40] if slot >= 40 else kv.at[h, slot]
+        sem = {40: 0, 41: 7}.get(slot, slot)
         return remote(src, dst, kv_ssem.at[h, sem], kv_rsem.at[h, sem], at_y(1 if up else NY - 1))
 
     for h in range(HEADS):
         hop(h, 1).start()
-        hop(h, 7).start()
+        hop(h, 6).start()
 
     for copy in [*get_own, *get_text, get_w, *get_small[2:]]:
         copy.start()
@@ -169,11 +164,14 @@
         for i in range(1, NH):
             f_hop(part, i).start()
 
-    for h in range(HEADS):
-        hop(h, 1).wait_recv()
-        hop(h, 2).start()
-        hop(h, 7).wait_recv()
-        hop(h, 6).start()
+    def relay(h, step):
+        for slot, on in (((1, 2), (6, 5)), ((2, 3), (5, 4)), ((3, 40), (4, 41)))[step - 1]:
+            hop(h, slot).wait_recv()
+            hop(h, on).start()
+
+    for h in range(HEADS):
+        relay(h, 1)
+    relay(0, 2)
 
     scale = math.log2(math.e) / math.sqrt(HD)
 
@@ -192,18 +190,17 @@
         for i in range(NH):
             if (r, i) != (0, 0):
                 q_hop(r, i).wait_recv()
-    for half in range(2):
+    def queries(half):
         for h in range(HEADS):
             rows = qraw[half, :, :, :, pl.ds(h * HD, HD)].reshape(PATCH, HD).astype(F32)
             qall[half, 0, h] = normed(rows, qg)
         for j in (2, 1, 3):
             x_hop(half, j).start()
 
-    for h in range(HEADS):
-        hop(h, 2).wait_recv()
-        hop(h, 3).start()
-        hop(h, 6).wait_recv()
-        hop(h, 5).start()
+    queries(0)
+    relay(1, 2)
+    relay(2, 2)
+    queries(1)
 
     for part in range(2):
         f_local[part].wait()
@@ -215,10 +212,7 @@
         kv[h, NEW, 1] = kvraw[1, :, :, cols].reshape(PATCH, HD)
 
     for h in range(HEADS):
-        hop(h, 3).wait_recv()
-        hop(h, 40).start()
-        hop(h, 5).wait_recv()
-        hop(h, 41).start()
+        relay(h, 3)
 
     for copy in get_own + get_text:
         copy.wait()
@@ -234,19 +228,29 @@
     def z_hop(half):
         return remote(zsend.at[half], zrecv.at[half], z_ssem.at[half], z_rsem.at[half], at_head(1, 0))
 
-    def attend(half, h):
+    def scan(half, h, slots):
         q = qall[half, :, h].reshape(NX * PATCH, HD)
-        keys = kv[h, pl.ds(1, NY), 0].reshape(NY * PATCH, HD)
-        values = kv[h, pl.ds(1, NY), 1].reshape(NY * PATCH, HD)
+        keys = kv[h, pl.ds(1, slots), 0].reshape(slots * PATCH, HD)
+        values = kv[h, pl.ds(1, slots), 1].reshape(slots * PATCH, HD)
         scores = dot_nt(q, keys)
-        split = (NY - 1) * PATCH
-        scores = jnp.concatenate([scores[:, :split], scores[:, split:] + bias], axis=1)
+        lo, hi = (TEXT - 1) * PATCH, TEXT * PATCH
+        ends = [scores[:, hi:]] if slots > TEXT else []
+        scores = jnp.concatenate([scores[:, :lo], scores[:, lo:hi] + bias, *ends], axis=1)
         mine = jnp.concatenate([dot_nt(q[:HALF], kv[h, NEW, 0]), dot_nt(q[HALF:], kv[h, OWN, 0])], axis=0)
         top = jnp.maximum(jnp.max(scores, axis=-1, keepdims=True), jnp.max(mine, axis=-1, keepdims=True))
         e = jnp.exp2((scores - top) * scale).astype(BF)
         e_mine = jnp.exp2((mine - top) * scale).astype(BF)
         own = [dot(e_mine[:HALF], with_ones(kv[h, NEW, 1])), dot(e_mine[HALF:], with_ones(kv[h, OWN, 1]))]
-        out = dot(e, with_ones(values)) + jnp.concatenate(own, axis=0)
+        return dot(e, with_ones(values)) + jnp.concatenate(own, axis=0), top
+
+    def scan_far(half, h, out, top):
+        q = qall[half, :, h].reshape(NX * PATCH, HD)
+        scores = dot_nt(q, kv[h, FAR, 0])
+        new_top = jnp.maximum(top, jnp.max(scores, axis=-1, keepdims=True))
+        e = jnp.exp2((scores - new_top) * scale).astype(BF)
+        return out * jnp.exp2((top - new_top) * scale) + dot(e, with_ones(kv[h, FAR, 1])), new_top
+
+    def keep(half, h, out, top):
         top = top * scale
         lane = lax.broadcasted_iota(jnp.int32, (PATCH, HD), 1)
         table = jnp.zeros((PATCH, HD), F32)
@@ -257,8 +261,11 @@
         stats = three_parts(jnp.transpose(table)[0:8])
         for j in range(NX):
             obuf[half, h, j, pl.ds(PATCH, STAT), :] = stats
-        for j in (2, 1, 3):
-            o_hop(half, h, j).start()
+
+    def send_out(half):
+        for h in range(HEADS):
+            for j in (2, 1, 3):
+                o_hop(half, h, j).start()
 
     def sources(half, h):
         refs = [obuf.at[half, h, 0]] + [orecv.at[half, h, j] for j in range(1, NX)]
@@ -272,6 +279,7 @@
         for h in range(HEADS):
             for j in range(1, NX):
                 o_hop(half, h, j).wait_recv()
+        for h in range(HEADS):
             parts, stats = sources(half, h)
             top, factors, total = shares(stats)
             out = dot(jnp.concatenate([diagonal(f, HALF) for f in factors], axis=1), parts)
@@ -331,14 +339,20 @@
                 def _():
                     pfin[c] = mine
 
-    for half in range(2):
-        for j in range(1, NX):
-            x_hop(half, j).wait_recv()
-        for h in range(HEADS):
-            if half == 0:
-                hop(h, 40).wait_recv()
-                hop(h, 41).wait_recv()
-            attend(half, h)
+    for j in range(1, NX):
+        x_hop(0, j).wait_recv()
+    partial = [scan(0, h, NY - 1) for h in range(HEADS)]
+    for h in range(HEADS):
+        hop(h, 40).wait_recv()
+        hop(h, 41).wait_recv()
+    for h in range(HEADS):
+        keep(0, h, *scan_far(0, h, *partial[h]))
+    send_out(0)
+    for j in range(1, NX):
+        x_hop(1, j).wait_recv()
+    for h in range(HEADS):
+        keep(1, h, *scan(1, h, NY))
+    send_out(1)
     merge_x(0)
     merge_x(1)
     merge_z(0)
@@ -367,7 +381,7 @@
             if i > 0:
                 f_hop(r, i).wait_send()
     for h in range(HEADS):
-        for slot in (1, 2, 3, 40, 41, 5, 6, 7):
+        for slot in (1, 2, 3, 4, 5, 6, 40, 41):
             hop(h, slot).wait_send()
     for half in range(2):
         for j in range(1, NX):

time: 62.9 us -> 64.5 us (1.025)
  Pallas kernels: 60.6 us -> 62.2 us
    pallas_call x1, Pallas kernels: 60.6 us -> 62.2 us  [on_device(): pl.pallas_call(kernel, out_shape=jax.ShapeDtypeStruct((TOK, D), BF), in_s...]
where the time goes in v4:
time: 64.5 us; the launch traced here: 64.4 us
  Pallas kernels  62.2 us (96%)
  local copies, waits for them, and re-layouts  1.54 us (2%)
  between operations  0.66 us (1%)
    pallas_call x1, Pallas kernels, on_device(): pl.pallas_call(kernel, out_shape=jax.ShapeDtypeStruct((TOK, D), BF), in_s...  62.2 us
    unnamed x1, local copies, waits for them, and re-layouts  1.54 us

profile of v4, /device:TPU:1, one launch (start us, length us, event | category | flops | bytes accessed | tf_op | source)
XLA Modules:
  0.0 64.4 jit_solution(10492189611859637909)
XLA Ops:
  0.7 62.2 %joint_attention.1 = bf16[16,3072]{1,0:T(8,128)(2,1)} custom-call(bf16[16,9216]{1,0:T(8,128)(2,1)} %fresh.1, bf16[2,128,384]{2,1,0:T(8,128)(2,1)} %stale.1, bf16[2,512,384]{2,1,0:T(8,128)(2,1)} %text.1, s32[1]{0:T(128)S(6)} %copy.11.tlen, f32[1,128]{1,0:T(1,128)} %bitcast.4, f32[1,128]{1,0:T(1,128)} %bitcast.5, bf16[384,3072]{1,0:T(8,128)(2,1)} %w.1, ...), custom_call_target="tpu_custom_call" | custom-call | flops 2000000000 | bytes 4000000 | tf_op jit(solution)/shard_map/joint_attention/pallas_call | solution.py:404
  62.9 1.5 %copy.12 = bf16[16,3072]{1,0:T(8,128)(2,1)} copy(bf16[16,3072]{1,0:T(8,128)(2,1)} %joint_attention.1) | data formatting | bytes 196608

commit v5 on v4

--- a/solution.py
+++ b/solution.py
@@ -17,7 +17,7 @@
 HALF = PATCH // 2
 TOK = PATCH // NH
 OWN, TEXT, FAR, NEW = 0, 7, 8, 9
-STAT = 32
+STAT = 16
 D = 3072
 CHUNKS = 3
 CW = D // CHUNKS
@@ -28,15 +28,19 @@
     return lax.dot_general(a, b, (((1,), (1,)), ((), ())), preferred_element_type=F32)
 
 
-def three_parts(rows):
+def stat_rows(top, total):
+    at = lax.broadcasted_iota(jnp.int32, (8, HD), 0)
+    rows = jnp.where(at < 3, top, total)
     hi = rows.astype(BF).astype(F32)
     mid = (rows - hi).astype(BF).astype(F32)
-    return jnp.concatenate([hi, mid, rows - hi - mid, jnp.zeros_like(rows)], axis=0).astype(BF)
-
-
-def whole(parts):
-    parts = parts.astype(F32)
-    return parts[0:8] + parts[8:16] + parts[16:24]
+    part = at % 3
+    rows = jnp.where(part == 0, hi, jnp.where(part == 1, mid, rows - hi - mid))
+    return jnp.concatenate([rows, jnp.zeros_like(rows)], axis=0).astype(BF)
+
+
+def whole(rows):
+    rows = rows.astype(F32)
+    return rows[0:1] + rows[1:2] + rows[2:3], rows[3:4] + rows[4:5] + rows[5:6]
 
 
 def with_ones(values):
@@ -228,14 +232,13 @@
     def z_hop(half):
         return remote(zsend.at[half], zrecv.at[half], z_ssem.at[half], z_rsem.at[half], at_head(1, 0))
 
-    def scan(half, h, slots):
+    def scan(half, h):
         q = qall[half, :, h].reshape(NX * PATCH, HD)
-        keys = kv[h, pl.ds(1, slots), 0].reshape(slots * PATCH, HD)
-        values = kv[h, pl.ds(1, slots), 1].reshape(slots * PATCH, HD)
+        keys = kv[h, pl.ds(1, NY), 0].reshape(NY * PATCH, HD)
+        values = kv[h, pl.ds(1, NY), 1].reshape(NY * PATCH, HD)
         scores = dot_nt(q, keys)
         lo, hi = (TEXT - 1) * PATCH, TEXT * PATCH
-        ends = [scores[:, hi:]] if slots > TEXT else []
-        scores = jnp.concatenate([scores[:, :lo], scores[:, lo:hi] + bias, *ends], axis=1)
+        scores = jnp.concatenate([scores[:, :lo], scores[:, lo:hi] + bias, scores[:, hi:]], axis=1)
         mine = jnp.concatenate([dot_nt(q[:HALF], kv[h, NEW, 0]), dot_nt(q[HALF:], kv[h, OWN, 0])], axis=0)
         top = jnp.maximum(jnp.max(scores, axis=-1, keepdims=True), jnp.max(mine, axis=-1, keepdims=True))
         e = jnp.exp2((scores - top) * scale).astype(BF)
@@ -243,14 +246,7 @@
         own = [dot(e_mine[:HALF], with_ones(kv[h, NEW, 1])), dot(e_mine[HALF:], with_ones(kv[h, OWN, 1]))]
         return dot(e, with_ones(values)) + jnp.concatenate(own, axis=0), top
 
-    def scan_far(half, h, out, top):
-        q = qall[half, :, h].reshape(NX * PATCH, HD)
-        scores = dot_nt(q, kv[h, FAR, 0])
-        new_top = jnp.maximum(top, jnp.max(scores, axis=-1, keepdims=True))
-        e = jnp.exp2((scores - new_top) * scale).astype(BF)
-        return out * jnp.exp2((top - new_top) * scale) + dot(e, with_ones(kv[h, FAR, 1])), new_top
-
-    def keep(half, h, out, top):
+    def send_out(half, h, out, top):
         top = top * scale
         lane = lax.broadcasted_iota(jnp.int32, (PATCH, HD), 1)
         table = jnp.zeros((PATCH, HD), F32)
@@ -258,21 +254,16 @@
             rows = slice(j * PATCH, (j + 1) * PATCH)
             obuf[half, h, j, pl.ds(0, PATCH), :] = out[rows, :HD].astype(BF)
             table = jnp.where(lane == j, top[rows], jnp.where(lane == NX + j, out[rows, HD:], table))
-        stats = three_parts(jnp.transpose(table)[0:8])
+        rows = jnp.transpose(table)[0:8]
         for j in range(NX):
+            stats = stat_rows(rows[j : j + 1], rows[NX + j : NX + j + 1])
             obuf[half, h, j, pl.ds(PATCH, STAT), :] = stats
-
-    def send_out(half):
-        for h in range(HEADS):
-            for j in (2, 1, 3):
-                o_hop(half, h, j).start()
+        for j in (2, 1, 3):
+            o_hop(half, h, j).start()
 
     def sources(half, h):
         refs = [obuf.at[half, h, 0]] + [orecv.at[half, h, j] for j in range(1, NX)]
-        stats = []
-        for j, ref in enumerate(refs):
-            rows, at = whole(ref[pl.ds(PATCH, STAT), :]), (NX - j) % NX
-            stats.append((rows[at : at + 1], rows[NX + at : NX + at + 1]))
+        stats = [whole(ref[pl.ds(PATCH, STAT), :]) for ref in refs]
         return jnp.concatenate([ref[pl.ds(0, PATCH), :] for ref in refs], axis=0), stats
 
     def merge_x(half):
@@ -284,17 +275,15 @@
             top, factors, total = shares(stats)
             out = dot(jnp.concatenate([diagonal(f, HALF) for f in factors], axis=1), parts)
             zsend[half, h, pl.ds(0, HALF), :] = out.astype(BF)
-            row = lax.broadcasted_iota(jnp.int32, (8, HD), 0)
-            table = jnp.where(row == 0, top, jnp.where(row == 1, total, 0.0))
-            zsend[half, h, pl.ds(HALF, STAT), :] = three_parts(pltpu.roll(table, HALF, 1))
+            top, total = (pltpu.roll(jnp.broadcast_to(row, (8, HD)), HALF, 1) for row in (top, total))
+            zsend[half, h, pl.ds(HALF, STAT), :] = stat_rows(top, total)
         z_hop(half).start()
 
     def merge_z(half):
         z_hop(half).wait_recv()
         for h in range(HEADS):
             parts, stats = sources(half, h)
-            far = whole(zrecv[half, h, pl.ds(HALF, STAT), :])
-            _, factors, total = shares(stats + [(far[0:1], far[1:2])])
+            _, factors, total = shares(stats + [whole(zrecv[half, h, pl.ds(HALF, STAT), :])])
             inverse = 1.0 / total
             weights = [diagonal(f * inverse, 0) for f in factors]
             out = dot(jnp.concatenate(weights[:NX], axis=1), parts)
@@ -341,18 +330,14 @@
 
     for j in range(1, NX):
         x_hop(0, j).wait_recv()
-    partial = [scan(0, h, NY - 1) for h in range(HEADS)]
     for h in range(HEADS):
         hop(h, 40).wait_recv()
         hop(h, 41).wait_recv()
-    for h in range(HEADS):
-        keep(0, h, *scan_far(0, h, *partial[h]))
-    send_out(0)
+        send_out(0, h, *scan(0, h))
     for j in range(1, NX):
         x_hop(1, j).wait_recv()
     for h in range(HEADS):
-        keep(1, h, *scan(1, h, NY))
-    send_out(1)
+        send_out(1, h, *scan(1, h))
     merge_x(0)
     merge_x(1)
     merge_z(0)

time: 64.5 us -> 61.6 us (0.955)
  Pallas kernels: 62.2 us -> 59.2 us
    pallas_call x1, Pallas kernels: 62.2 us -> 59.2 us  [on_device(): pl.pallas_call(kernel, out_shape=jax.ShapeDtypeStruct((TOK, D), BF), in_s...]
where the time goes in v5:
time: 61.6 us; the launch traced here: 61.4 us
  Pallas kernels  59.2 us (96%)
  local copies, waits for them, and re-layouts  1.54 us (2%)
  between operations  0.66 us (1%)
    pallas_call x1, Pallas kernels, on_device(): pl.pallas_call(kernel, out_shape=jax.ShapeDtypeStruct((TOK, D), BF), in_s...  59.2 us
    unnamed x1, local copies, waits for them, and re-layouts  1.54 us

profile of v5, /device:TPU:1, one launch (start us, length us, event | category | flops | bytes accessed | tf_op | source)
XLA Modules:
  0.0 61.4 jit_solution(18309026631507918174)
XLA Ops:
  0.7 59.2 %joint_attention.1 = bf16[16,3072]{1,0:T(8,128)(2,1)} custom-call(bf16[16,9216]{1,0:T(8,128)(2,1)} %fresh.1, bf16[2,128,384]{2,1,0:T(8,128)(2,1)} %stale.1, bf16[2,512,384]{2,1,0:T(8,128)(2,1)} %text.1, s32[1]{0:T(128)S(6)} %copy.11.tlen, f32[1,128]{1,0:T(1,128)} %bitcast.4, f32[1,128]{1,0:T(1,128)} %bitcast.5, bf16[384,3072]{1,0:T(8,128)(2,1)} %w.1, ...), custom_call_target="tpu_custom_call" | custom-call | flops 2000000000 | bytes 4000000 | tf_op jit(solution)/shard_map/joint_attention/pallas_call | solution.py:389
  59.8 1.5 %copy.12 = bf16[16,3072]{1,0:T(8,128)(2,1)} copy(bf16[16,3072]{1,0:T(8,128)(2,1)} %joint_attention.1) | data formatting | bytes 196608

commit v6 on v5

--- a/solution.py
+++ b/solution.py
@@ -229,8 +229,10 @@
             obuf.at[half, h, j], orecv.at[half, h, NX - j], o_ssem.at[half, h, j], o_rsem.at[half, h, NX - j], at_x(j)
         )
 
-    def z_hop(half):
-        return remote(zsend.at[half], zrecv.at[half], z_ssem.at[half], z_rsem.at[half], at_head(1, 0))
+    def z_hop(half, h):
+        return remote(
+            zsend.at[half, h], zrecv.at[half, h], z_ssem.at[half, h], z_rsem.at[half, h], at_head(1, 0)
+        )
 
     def scan(half, h):
         q = qall[half, :, h].reshape(NX * PATCH, HD)
@@ -270,18 +272,17 @@
         for h in range(HEADS):
             for j in range(1, NX):
                 o_hop(half, h, j).wait_recv()
-        for h in range(HEADS):
             parts, stats = sources(half, h)
             top, factors, total = shares(stats)
             out = dot(jnp.concatenate([diagonal(f, HALF) for f in factors], axis=1), parts)
             zsend[half, h, pl.ds(0, HALF), :] = out.astype(BF)
             top, total = (pltpu.roll(jnp.broadcast_to(row, (8, HD)), HALF, 1) for row in (top, total))
             zsend[half, h, pl.ds(HALF, STAT), :] = stat_rows(top, total)
-        z_hop(half).start()
+            z_hop(half, h).start()
 
     def merge_z(half):
-        z_hop(half).wait_recv()
         for h in range(HEADS):
+            z_hop(half, h).wait_recv()
             parts, stats = sources(half, h)
             _, factors, total = shares(stats + [whole(zrecv[half, h, pl.ds(HALF, STAT), :])])
             inverse = 1.0 / total
@@ -373,7 +374,8 @@
             x_hop(half, j).wait_send()
             for h in range(HEADS):
                 o_hop(half, h, j).wait_send()
-        z_hop(half).wait_send()
+        for h in range(HEADS):
+            z_hop(half, h).wait_send()
         for c in range(CHUNKS):
             p_hop(half, c).wait_send()
             for n in range(2):
@@ -413,7 +415,8 @@
             pltpu.VMEM((TOK, D), BF),
             pltpu.VMEM((1, D), F32),
             dma((6 + 2 * HEADS,)), dma((NZ, NH)), dma((NZ, NH)), dma((2, NH)), dma((2, NH)), dma((HEADS, NY)),
-            dma((HEADS, NY)), dma((2, NX)), dma((2, NX)), dma((2, HEADS, NX)), dma((2, HEADS, NX)), dma((2,)), dma((2,)),
+            dma((HEADS, NY)), dma((2, NX)), dma((2, NX)), dma((2, HEADS, NX)), dma((2, HEADS, NX)), dma((2, HEADS)),
+            dma((2, HEADS)),
             dma((2, CHUNKS)), dma((2, CHUNKS)), dma((2, CHUNKS, 2)), dma((CHUNKS, NL)),
         ],
         name="joint_attention",

time: 61.6 us -> 61.3 us (level)
  no operation moved by 1% of the time
where the time goes in v6:
time: 61.3 us; the launch traced here: 61.2 us
  Pallas kernels  59 us (96%)
  local copies, waits for them, and re-layouts  1.54 us (3%)
  between operations  0.66 us (1%)
    pallas_call x1, Pallas kernels, on_device(): pl.pallas_call(kernel, out_shape=jax.ShapeDtypeStruct((TOK, D), BF), in_s...  59 us
    unnamed x1, local copies, waits for them, and re-layouts  1.54 us

profile of v6, /device:TPU:1, one launch (start us, length us, event | category | flops | bytes accessed | tf_op | source)
XLA Modules:
  0.0 61.2 jit_solution(2815517570833555235)
XLA Ops:
  0.7 59.0 %joint_attention.1 = bf16[16,3072]{1,0:T(8,128)(2,1)} custom-call(bf16[16,9216]{1,0:T(8,128)(2,1)} %fresh.1, bf16[2,128,384]{2,1,0:T(8,128)(2,1)} %stale.1, bf16[2,512,384]{2,1,0:T(8,128)(2,1)} %text.1, s32[1]{0:T(128)S(6)} %copy.11.tlen, f32[1,128]{1,0:T(1,128)} %bitcast.4, f32[1,128]{1,0:T(1,128)} %bitcast.5, bf16[384,3072]{1,0:T(8,128)(2,1)} %w.1, ...), custom_call_target="tpu_custom_call" | custom-call | flops 2000000000 | bytes 4000000 | tf_op jit(solution)/shard_map/joint_attention/pallas_call | solution.py:391
  59.6 1.5 %copy.12 = bf16[16,3072]{1,0:T(8,128)(2,1)} copy(bf16[16,3072]{1,0:T(8,128)(2,1)} %joint_attention.1) | data formatting | bytes 196608
